TPU v7x, 128 devices: a whole 4x4x4 slice. The times are simulated.
128 devices in a mesh: dp: 16 (over z, x), expert: 8 (over y, core).
Axes of the slice: x: 4, y: 4, z: 4, core: 2. Of those that a mesh axis runs over, the one named last changes fastest.
Arguments:
- local_grads: bfloat16 [16, 8, 4, 1048576], P('dp', 'expert')
- master_weights: float32 [8, 4, 1048576], P('expert', None, 'dp'), may hold values from -6 to 6
- first_moment: float32 [8, 4, 1048576], P('expert', None, 'dp')
- second_moment: float32 [8, 4, 1048576], P('expert', None, 'dp')
Outputs:
- new_params: bfloat16 [8, 4, 1048576], P('expert')
- new_master: float32 [8, 4, 1048576], P('expert', None, 'dp')
- new_first: float32 [8, 4, 1048576], P('expert', None, 'dp')
- new_second: float32 [8, 4, 1048576], P('expert', None, 'dp')
All inputs are finite; a program needn't handle non-finite values.
Results may differ from a plain program's by a relative error of at most 0.0013.
Values may be sent and summed in bfloat16 or wider, within the bound.
No kernel may reach another device: no remote copies, remote signals or barrier semaphores. Data moves between devices by JAX's collectives and lax.ppermute only.
A program may use at most 128 MiB of HBM per device.

v0:
```python
import functools
import jax
import jax.numpy as jnp
from jax import lax
from jax.sharding import Mesh
from jax.sharding import PartitionSpec as P

DP = ("dp_0", "dp_1")
DP_EXPERT = ("dp_0", "dp_1", "expert_0", "expert_1")
EXPERT = ("expert_0", "expert_1")
beta_first = 0.9
beta_second = 0.95
correct_first = 1.0 - 0.9**10
correct_second = 1.0 - 0.95**10
learn_rate = 0.05
decay_rate = 0.1
clip_limit = 1.0
tiny_eps = 1e-08
norm_eps = 1e-06


def by_axis(x, axes):
    return functools.reduce(lax.psum, axes, x)


def adam_update(gradient, master, first, second, clip_factor):
    scaled = clip_factor * gradient
    new_first = beta_first * first + (1.0 - beta_first) * scaled
    new_second = beta_second * second + (1.0 - beta_second) * scaled * scaled
    direction = new_first / correct_first / (jnp.sqrt(new_second / correct_second) + tiny_eps)
    new_master = master - learn_rate * (decay_rate * master + direction)
    return (new_master, new_first, new_second)


def shards(local_grads, master_weights, first_moment, second_moment):
    replicas = lax.axis_size(DP)
    own_grads = local_grads[0, 0]
    layer_count = own_grads.shape[0]
    share = own_grads.shape[1] // replicas
    pieces_all = own_grads.reshape(layer_count, replicas, share)
    arrived = lax.all_to_all(pieces_all, DP, split_axis=1, concat_axis=1, tiled=True)
    reduced = jnp.sum(arrived.astype(jnp.float32), axis=1)
    mean_grad = reduced / replicas
    squares = jnp.sum(mean_grad * mean_grad)
    total_squares = by_axis(squares, DP_EXPERT)
    grad_norm = jnp.sqrt(total_squares)
    clip_factor = jnp.minimum(1.0, clip_limit / (grad_norm + norm_eps))
    new_master, new_first, new_second = adam_update(
        mean_grad, master_weights[0], first_moment[0], second_moment[0], clip_factor
    )
    rounded = new_master.astype(jnp.bfloat16)
    gathered = lax.all_gather(rounded, DP, axis=1, tiled=True)
    return (gathered[None], new_master[None], new_first[None], new_second[None])


def solution(mesh):
    torus = Mesh(mesh.devices.reshape(4, 4, 4, 2), ("dp_0", "dp_1", "expert_0", "expert_1"))
    return jax.shard_map(
        shards,
        mesh=torus,
        in_specs=(
            P(DP, EXPERT, None, None),
            P(EXPERT, None, DP),
            P(EXPERT, None, DP),
            P(EXPERT, None, DP),
        ),
        out_specs=(
            P(EXPERT, None, None),
            P(EXPERT, None, DP),
            P(EXPERT, None, DP),
            P(EXPERT, None, DP),
        ),
        check_vma=False,
    )
```

profile of v0, /device:TPU:1, one launch (start us, length us, event | category | flops | bytes accessed | tf_op | source)
XLA Modules:
  0.0 238.8 jit_solution(16362549095326047776)
XLA Ops:
  7.2 0.0 all-gather.2.cloned.1.call-start
  7.2 103.3 %all_to_all.5 = bf16[4,16,65536]{2,0,1:T(4,128)(2,1)} all-to-all(bf16[4,16,65536]{2,0,1:T(4,128)(2,1)} %bitcast.32), channel_id=1, replica_groups=mesh['dp_0'=4,'dp_1'=4,'expert_0'=4,'expert_1'=2] {'dp_0','dp_1'}, dimensions={1} | all-to-all | bytes 16777216 | tf_op jit(solution)/shard_map/all_to_all | solution.py:41
  110.5 0.0 copy-start
  110.5 0.0 copy-start.1
  110.5 7.2 %convert_reduce_fusion = f32[4,65536]{1,0:T(4,128)S(1)} fusion(bf16[4,16,65536]{2,0,1:T(4,128)(2,1)} %all_to_all.5), kind=kLoop, calls=%fused_computation | loop fusion | flops 8126464 | bytes 9437184 | tf_op jit(solution)/shard_map/reduce_sum | solution.py:42
  117.8 1.1 multiply_reduce_fusion
  118.9 7.3 %psum.28 = f32[]{:T(128)} all-reduce(f32[]{:T(128)} %multiply_reduce_fusion), channel_id=1, replica_groups=mesh['dp_0'=4,'dp_1'=4,'expert_0'=4,'expert_1'=2] {'dp_0'}, use_global_device_ids=true, to_apply=%region_2.0 | all-reduce | flops 1 | bytes 8 | tf_op jit(solution)/shard_map/psum | solution.py:23
  126.3 7.2 %psum.29 = f32[]{:T(128)} all-reduce(f32[]{:T(128)} %psum.28), channel_id=1, replica_groups=mesh['dp_0'=4,'dp_1'=4,'expert_0'=4,'expert_1'=2] {'dp_1'}, use_global_device_ids=true, to_apply=%region_3.0 | all-reduce | flops 1 | bytes 8 | tf_op jit(solution)/shard_map/psum | solution.py:23
  133.4 9.3 %psum.30 = f32[]{:T(128)} all-reduce(f32[]{:T(128)} %psum.29), channel_id=1, replica_groups=mesh['dp_0'=4,'dp_1'=4,'expert_0'=4,'expert_1'=2] {'expert_0'}, use_global_device_ids=true, to_apply=%region_4.0 | all-reduce | flops 1 | bytes 8 | tf_op jit(solution)/shard_map/psum | solution.py:23
  142.8 10.6 %psum.31 = f32[]{:T(128)} all-reduce(f32[]{:T(128)} %psum.30), channel_id=1, replica_groups=mesh['dp_0'=4,'dp_1'=4,'expert_0'=4,'expert_1'=2] {'expert_1'}, use_global_device_ids=true, to_apply=%region_5.0 | all-reduce | flops 1 | bytes 8 | tf_op jit(solution)/shard_map/psum | solution.py:23
  154.1 0.0 copy-done
  154.1 0.0 copy-done.1
  154.1 3.7 %fusion.10 = bf16[4,65536]{1,0:T(4,128)(2,1)} fusion(f32[1,4,65536]{2,1,0:T(4,128)S(1)} %copy-done, f32[1,4,65536]{2,1,0:T(4,128)S(1)} %copy-done.1, f32[1,4,65536]{2,1,0:T(4,128)} %param.6, f32[4,65536]{1,0:T(4,128)S(1)} %convert_reduce_fusion, f32[]{:T(128)S(6)} %mul.104), kind=kLoop, calls=%fused_computation.17 | loop fusion | flops 4456448 | bytes 4718596 | tf_op jit(solution)/shard_map/convert_element_type | solution.py:51
  157.9 0.0 all-gather.2.cloned.1.call-update
  157.9 4.5 %multiply_subtract_fusion = (f32[1,4,65536]{2,1,0:T(4,128)}, f32[1,4,65536]{2,1,0:T(4,128)}, f32[1,4,65536]{2,1,0:T(4,128)}) fusion(f32[1,4,65536]{2,1,0:T(4,128)S(1)} %copy-done, f32[4,65536]{1,0:T(4,128)S(1)} %convert_reduce_fusion, f32[]{:T(128)S(6)} %mul.104, f32[1,4,65536]{2,1,0:T(4,128)} %param.6, f32[1,4,65536]{2,1,0:T(4,128)S(1)} %copy-done.1), kind=kLoop, calls=%fused_computation.18 | loop fusion | flops 4194304 | bytes 7340036 | tf_op jit(solution)/shard_map/sub | solution.py:31
  162.3 61.5 %all-gather.2.cloned.1.call-done = bf16[4,1048576]{1,0:T(4,128)(2,1)} async-done(((bf16[4,65536]{1,0:T(4,128)(2,1)}), bf16[4,1048576]{1,0:T(4,128)(2,1)}) %all-gather.2.cloned.1.call-update) | async-done | bytes 8388624 | tf_op jit(solution)/shard_map/all_gather | solution.py:52
  223.9 8.1 %copy.9 = bf16[1,4,1048576]{2,1,0:T(4,128)(2,1)} copy(bf16[1,4,1048576]{2,1,0:T(4,128)(2,1)} %bitcast.33) | data formatting | bytes 16777216
Async XLA Ops:
  7.2 216.7 %all-gather.2.cloned.1.call-start = ((), (), s32[]{:S(2)}) async-start(), calls=%async_computation.1 | async-start | bytes 8912896 | tf_op jit(solution)/shard_map/all_gather | solution.py:52
  110.5 43.6 %copy-start = (f32[1,4,65536]{2,1,0:T(4,128)S(1)}, f32[1,4,65536]{2,1,0:T(4,128)}, u32[]{:S(2)}) copy-start(f32[1,4,65536]{2,1,0:T(4,128)} %param.5) | copy-start | bytes 3145732
  110.5 43.6 %copy-start.1 = (f32[1,4,65536]{2,1,0:T(4,128)S(1)}, f32[1,4,65536]{2,1,0:T(4,128)}, u32[]{:S(2)}) copy-start(f32[1,4,65536]{2,1,0:T(4,128)} %param.7) | copy-start | bytes 3145732
Sparse Core Ops, SparseCore 0:
  158.0 65.8 all-gather.1
where the time goes:
time: 239 us
  blocking collectives  138 us (58%)
  waiting for transfers between devices  61.5 us (26%)
  other arithmetic  16.6 us (7%)
  between operations  14.8 us (6%)
  local copies, waits for them, and re-layouts  8.06 us (3%)
    all_to_all x1, blocking collectives, shards(): lax.all_to_all(pieces_all, DP, split_axis=1, concat_axis=1, tiled=True)  103 us
    all_gather x1, waiting for transfers between devices, shards(): gathered = lax.all_gather(rounded, DP, axis=1, tiled=True)  61.5 us
    psum x4, blocking collectives, by_axis(): return functools.reduce(lax.psum, axes, x)  34.5 us
    unnamed x5, local copies, waits for them, and re-layouts  8.06 us
    reduce_sum x1, other arithmetic, shards(): reduced = jnp.sum(arrived.astype(jnp.float32), axis=1)  7.25 us
  transfers between devices with their start and end apart: 1, of which 1 were waited for; matrix products, arithmetic and copies ran while one was open for 2% of the time, Pallas kernels for 0%

commit v1 on v0

--- a/solution.py
+++ b/solution.py
@@ -49,7 +49,11 @@
         mean_grad, master_weights[0], first_moment[0], second_moment[0], clip_factor
     )
     rounded = new_master.astype(jnp.bfloat16)
-    gathered = lax.all_gather(rounded, DP, axis=1, tiled=True)
+    outcome_arr = lax.axis_size(DP)
+    shaped = lax.all_to_all(
+        jnp.stack([rounded] * outcome_arr, axis=0), axis_name=DP, split_axis=0, concat_axis=0
+    )
+    gathered = jnp.concatenate(shaped, axis=1)
     return (gathered[None], new_master[None], new_first[None], new_second[None])
 
 

time: 239 us -> 262 us (1.096)
  blocking collectives: 138 us -> 238 us
  waiting for transfers between devices: 61.5 us -> 0 us
  between operations: 14.8 us -> 1.38 us
  other arithmetic: 16.6 us -> 13.1 us
    all_to_all x0 -> x1, blocking collectives: none -> 99.8 us  [shards(): lax.all_to_all(jnp.stack([rounded] * outcome_arr, axis=0), axis_name=DP,...]
    all_gather x1 -> x0, waiting for transfers between devices: 61.5 us -> none  [shards(): gathered = lax.all_gather(rounded, DP, axis=1, tiled=True)]
    another operation x0 -> x1, local copies, waits for them, and re-layouts: none -> 6.63 us  [shards(): jnp.stack([rounded] * outcome_arr, axis=0)]
    another operation x0 -> x1, other arithmetic: none -> 4.79 us  [shards(): jnp.stack([rounded] * outcome_arr, axis=0)]
    unnamed x5 -> x3, local copies, waits for them, and re-layouts: 8.06 us -> 3.4 us
    sub x1 -> x0, other arithmetic: 4.45 us -> none  [adam_update(): new_master = master - learn_rate * (decay_rate * master + direction)]
    convert_element_type x1 -> x0, other arithmetic: 3.72 us -> none  [shards(): rounded = new_master.astype(jnp.bfloat16)]
  transfers between devices with their start and end apart: 1 -> 0, of which waited for: 1 -> 0; matrix products, arithmetic and copies ran while one was open for 2% -> 0% of each run, Pallas kernels for 0% -> 0%
where the time goes in v1:
time: 262 us
  blocking collectives  238 us (91%)
  other arithmetic  13.1 us (5%)
  local copies, waits for them, and re-layouts  10 us (4%)
    all_to_all x1, blocking collectives, shards(): lax.all_to_all(pieces_all, DP, split_axis=1, concat_axis=1, tiled=True)  103 us
    all_to_all x1, blocking collectives, shards(): lax.all_to_all(jnp.stack([rounded] * outcome_arr, axis=0), axis_name=DP,...  99.8 us
    psum x4, blocking collectives, by_axis(): return functools.reduce(lax.psum, axes, x)  34.5 us
    reduce_sum x1, other arithmetic, shards(): reduced = jnp.sum(arrived.astype(jnp.float32), axis=1)  7.19 us
    another operation x1, local copies, waits for them, and re-layouts, shards(): jnp.stack([rounded] * outcome_arr, axis=0)  6.63 us

profile of v1, /device:TPU:1, one launch (start us, length us, event | category | flops | bytes accessed | tf_op | source)
XLA Modules:
  0.0 262.1 jit_solution(15066226098057949123)
XLA Ops:
  0.6 103.3 %all_to_all.10 = bf16[4,16,65536]{2,0,1:T(4,128)(2,1)} all-to-all(bf16[4,16,65536]{2,0,1:T(4,128)(2,1)} %bitcast.14), channel_id=1, replica_groups=mesh['dp_0'=4,'dp_1'=4,'expert_0'=4,'expert_1'=2] {'dp_0','dp_1'}, dimensions={1} | all-to-all | bytes 16777216 | tf_op jit(solution)/shard_map/all_to_all | solution.py:41
  103.9 0.0 copy-start
  104.0 7.2 %convert_reduce_fusion = f32[4,65536]{1,0:T(4,128)S(1)} fusion(bf16[4,16,65536]{2,0,1:T(4,128)(2,1)} %all_to_all.10), kind=kLoop, calls=%fused_computation | loop fusion | flops 8126464 | bytes 9437184 | tf_op jit(solution)/shard_map/reduce_sum | solution.py:42
  111.1 1.1 multiply_reduce_fusion
  112.3 7.3 %psum.28 = f32[]{:T(128)} all-reduce(f32[]{:T(128)} %multiply_reduce_fusion), channel_id=1, replica_groups=mesh['dp_0'=4,'dp_1'=4,'expert_0'=4,'expert_1'=2] {'dp_0'}, use_global_device_ids=true, to_apply=%region_2.0 | all-reduce | flops 1 | bytes 8 | tf_op jit(solution)/shard_map/psum | solution.py:23
  119.6 7.2 %psum.29 = f32[]{:T(128)} all-reduce(f32[]{:T(128)} %psum.28), channel_id=1, replica_groups=mesh['dp_0'=4,'dp_1'=4,'expert_0'=4,'expert_1'=2] {'dp_1'}, use_global_device_ids=true, to_apply=%region_3.0 | all-reduce | flops 1 | bytes 8 | tf_op jit(solution)/shard_map/psum | solution.py:23
  126.8 9.3 %psum.30 = f32[]{:T(128)} all-reduce(f32[]{:T(128)} %psum.29), channel_id=1, replica_groups=mesh['dp_0'=4,'dp_1'=4,'expert_0'=4,'expert_1'=2] {'expert_0'}, use_global_device_ids=true, to_apply=%region_4.0 | all-reduce | flops 1 | bytes 8 | tf_op jit(solution)/shard_map/psum | solution.py:23
  136.1 10.6 %psum.31 = f32[]{:T(128)} all-reduce(f32[]{:T(128)} %psum.30), channel_id=1, replica_groups=mesh['dp_0'=4,'dp_1'=4,'expert_0'=4,'expert_1'=2] {'expert_1'}, use_global_device_ids=true, to_apply=%region_5.0 | all-reduce | flops 1 | bytes 8 | tf_op jit(solution)/shard_map/psum | solution.py:23
  147.5 0.0 copy-done
  147.5 4.8 %convert_bitcast_fusion = (bf16[4,65536]{1,0:T(4,128)(2,1)S(1)}, f32[1,4,65536]{2,1,0:T(4,128)}, f32[1,4,65536]{2,1,0:T(4,128)}, f32[1,4,65536]{2,1,0:T(4,128)}) fusion(f32[1,4,65536]{2,1,0:T(4,128)S(1)} %copy-done, f32[4,65536]{1,0:T(4,128)S(1)} %convert_reduce_fusion, f32[]{:T(128)S(6)} %mul.95, f32[1,4,65536]{2,1,0:T(4,128)} %param.6, f32[1,4,65536]{2,1,0:T(4,128)} %param.7), kind=kLoop, calls=%fused_computation.7 | loop fusion | flops 4456448 | bytes 7864324 | tf_op jit(solution)/shard_map/stack | solution.py:54
  152.3 6.6 %stack.5 = bf16[16,4,65536]{2,1,0:T(4,128)(2,1)} broadcast(bf16[4,65536]{1,0:T(4,128)(2,1)S(1)} %get-tuple-element.4), dimensions={1,2} | broadcast | bytes 8912896 | tf_op jit(solution)/shard_map/stack | solution.py:54
  158.9 99.8 %all_to_all.11 = bf16[16,4,65536]{2,1,0:T(4,128)(2,1)S(1)} all-to-all(bf16[16,4,65536]{2,1,0:T(4,128)(2,1)} %stack.5), channel_id=1, replica_groups=mesh['dp_0'=4,'dp_1'=4,'expert_0'=4,'expert_1'=2] {'dp_0','dp_1'}, dimensions={0} | all-to-all | bytes 16777216 | tf_op jit(solution)/shard_map/all_to_all | solution.py:53
  258.7 3.4 %copy.9 = bf16[1,4,1048576]{2,1,0:T(4,128)(2,1)} copy(bf16[1,4,1048576]{2,1,0:T(4,128)(2,1)S(1)} %bitcast.13) | data formatting | bytes 16777216
Async XLA Ops:
  103.9 43.5 %copy-start = (f32[1,4,65536]{2,1,0:T(4,128)S(1)}, f32[1,4,65536]{2,1,0:T(4,128)}, u32[]{:S(2)}) copy-start(f32[1,4,65536]{2,1,0:T(4,128)} %param.5) | copy-start | bytes 3145732
